TPU v7x, 32 devices: a whole 2x2x4 slice. The times are simulated.
32 devices in a mesh: parts: 2 (over y), tp: 16 (over z, x, core).
Axes of the slice: x: 2, y: 2, z: 4, core: 2. Of those that a mesh axis runs over, the one named last changes fastest.
Arguments:
- inputs: bfloat16 [512, 5120], P(('parts', 'tp')), parts along dimension 0, may hold values from -6 to 6
- out_grads: bfloat16 [2, 512, 25600], P(None, 'parts', 'tp'), parts along dimension 1, may hold values from -6 to 6
- frozen_weights: bfloat16 [2, 25600, 5120], P(None, 'tp'), may hold values from -0.078125 to 0.078125
- adapter_first: bfloat16 [2, 512, 5120], P(None, ('parts', 'tp')), parts along dimension 1, may hold values from -0.078125 to 0.078125
- adapter_second: bfloat16 [2, 512, 25600], P(None, ('parts', 'tp')), parts along dimension 1, may hold values from -0.3125 to 0.3125
- group_jobs: int32 [8], P('parts'), parts along dimension 0, may hold values from 0 to 3, each once
- owner_map: int32 [32], P('parts'), parts along dimension 0, may hold values from 0 to 15, each once
- segment_offsets: int32 [10], P('parts'), parts along dimension 0, may hold values from 0 to 256, as said below
- segment_lengths: int32 [8], P('parts'), parts along dimension 0, may hold values from 1 to 120, as said below
Outputs:
- input_grads: float32 [512, 5120], P(('parts', 'tp')), parts along dimension 0
- first_factor_gradient: float32 [2, 512, 5120], P(None, ('parts', 'tp')), parts along dimension 1
- second_factor_gradient: float32 [2, 512, 25600], P(None, ('parts', 'tp')), parts along dimension 1
There are 2 independent parts, one for each index of `parts`. A program takes and returns all parts, laid end to end along the dimension named above; an argument that names none is the same for every part. Nothing has to cross between parts.
Inputs may be any that keep to these rules, and one draw needn't show every extreme that they name: `group_jobs`: every job appears in exactly one slot. Device owner_map[j * 4 + q] stores rank rows q * 16 to (q + 1) * 16 - 1 of job j, at its local rows in that order; every device stores one piece. `segment_offsets`: starts at 0, rises strictly in multiples of 8, the last entry is 256. Slot s has segment_lengths[s] live tokens from segment_offsets[s] on; fewer than 8 positions of its padded span are padding. One slot in every draw has the largest length, with no padding.
All inputs are finite; a program needn't handle non-finite values.
Results may differ from a plain program's by a relative error of at most 0.003.
Values may be sent and summed in bfloat16 or wider, within the bound.
A program may use at most 192 MiB of HBM per device.

v0:
```python
import jax
import jax.numpy as jnp
from jax import lax
from jax.sharding import PartitionSpec as P

R = 64
SPLIT = 4
BLK = 8


adapter_scale = 0.5


def shards(
    inputs,
    out_grads,
    frozen_weights,
    adapter_first,
    adapter_second,
    group_jobs,
    owner_map,
    segment_offsets,
    segment_lengths,
):
    devices = lax.axis_size("tp")
    column_index = lax.axis_index("tp")
    job_count = group_jobs.shape[0]
    gradient_total = out_grads.shape[1]
    hidden_cols = out_grads.shape[2]
    width_columns = inputs.shape[1] // devices
    piece_rows = adapter_first.shape[1]
    blocks = gradient_total // BLK
    positions = jnp.arange(gradient_total, dtype=jnp.int32)
    slot_ids = jnp.arange(job_count, dtype=jnp.int32)
    slot_of = jnp.sum(
        (positions[:, None] >= segment_offsets[1:job_count][None, :]).astype(jnp.int32), axis=1
    )
    onehot = slot_of[:, None] == slot_ids[None, :]
    starts = jnp.sum(jnp.where(onehot, segment_offsets[:job_count][None, :], 0), axis=1)
    spans = jnp.sum(jnp.where(onehot, segment_lengths[None, :], 0), axis=1)
    live_mask = positions - starts < spans
    masked = out_grads * live_mask[None, :, None].astype(out_grads.dtype)
    pieces = owner_map.reshape(job_count, SPLIT)[group_jobs]
    within = jnp.arange(piece_rows, dtype=jnp.int32)
    rows_flat = (pieces[:, :, None] * piece_rows + within[None, None, :]).reshape(-1)
    received_first, received_second = (
        lax.all_to_all(adapter_first, "tp", split_axis=2, concat_axis=1, tiled=True),
        lax.all_to_all(adapter_second, "tp", split_axis=2, concat_axis=1, tiled=True),
    )
    slot_first = jnp.take(received_first, rows_flat, axis=1).reshape(2, job_count, R, width_columns)
    slot_second = jnp.take(received_second, rows_flat, axis=1).reshape(2, job_count, R, hidden_cols)
    block_slot = slot_of[::BLK]
    block_first = jnp.take(slot_first, block_slot, axis=1)
    block_second = jnp.take(slot_second, block_slot, axis=1)
    whole = lax.all_gather(inputs, "tp", axis=0, tiled=True)
    input_cols = lax.dynamic_slice_in_dim(whole, column_index * width_columns, width_columns, 1)
    column_blocks = input_cols.reshape(blocks, BLK, width_columns)
    grad_blocks = masked.reshape(2, blocks, BLK, hidden_cols)
    low_part = jnp.einsum(
        "nbd,pnrd->pnbr", column_blocks, block_first, preferred_element_type=jnp.float32
    )
    back_part = jnp.einsum(
        "pnbf,pnrf->pnbr", grad_blocks, block_second, preferred_element_type=jnp.float32
    )
    rank_projection, rank_backward = lax.psum((low_part, back_part), "tp")
    low_narrow = rank_projection.astype(jnp.bfloat16)
    back_narrow = rank_backward.astype(jnp.bfloat16)
    adapter_columns = adapter_scale * jnp.einsum(
        "pnbr,pnrd->nbd", back_narrow, block_first, preferred_element_type=jnp.float32
    )
    adapter_columns = adapter_columns.reshape(gradient_total, width_columns)
    frozen_product = jnp.einsum(
        "ptf,pfd->td", masked, frozen_weights, preferred_element_type=jnp.float32
    )
    placed = lax.dynamic_update_slice_in_dim(
        jnp.zeros_like(frozen_product), adapter_columns, column_index * width_columns, 1
    )
    input_grads = lax.psum_scatter(frozen_product + placed, "tp", scatter_dimension=0, tiled=True)
    block_onehot = (block_slot[:, None] == slot_ids[None, :]).astype(jnp.float32)
    first_terms = jnp.einsum(
        "pnbr,nbd->pnrd", back_narrow, column_blocks, preferred_element_type=jnp.float32
    )
    second_terms = jnp.einsum(
        "pnbr,pnbf->pnrf", low_narrow, grad_blocks, preferred_element_type=jnp.float32
    )
    slot_first_gradient = adapter_scale * jnp.einsum(
        "ns,pnrd->psrd", block_onehot, first_terms, precision=lax.Precision.HIGHEST
    )
    slot_second_gradient = adapter_scale * jnp.einsum(
        "ns,pnrf->psrf", block_onehot, second_terms, precision=lax.Precision.HIGHEST
    )
    local_first = jnp.zeros((2, devices * piece_rows, width_columns), jnp.float32)
    local_first = local_first.at[:, rows_flat].set(
        slot_first_gradient.reshape(2, job_count * R, width_columns)
    )
    local_second = jnp.zeros((2, devices * piece_rows, hidden_cols), jnp.float32)
    local_second = local_second.at[:, rows_flat].set(
        slot_second_gradient.reshape(2, job_count * R, hidden_cols)
    )
    first_factor_gradient, second_factor_gradient = (
        lax.all_to_all(local_first, "tp", split_axis=1, concat_axis=2, tiled=True),
        lax.all_to_all(local_second, "tp", split_axis=1, concat_axis=2, tiled=True),
    )
    return (input_grads, first_factor_gradient, second_factor_gradient)


def solution(mesh):
    return jax.shard_map(
        shards,
        mesh=mesh,
        in_specs=(
            P(("parts", "tp"), None),
            P(None, "parts", "tp"),
            P(None, "tp", None),
            P(None, ("parts", "tp"), None),
            P(None, ("parts", "tp"), None),
            P("parts"),
            P("parts"),
            P("parts"),
            P("parts"),
        ),
        out_specs=(
            P(("parts", "tp"), None),
            P(None, ("parts", "tp"), None),
            P(None, ("parts", "tp"), None),
        ),
        check_vma=False,
    )
```

profile of v0, /device:TPU:11, one launch (start us, length us, event | category | flops | bytes accessed | tf_op | source)
XLA Modules:
  0.0 470.3 jit_solution(17524767667820592893)
XLA Ops:
  7.2 0.0 copy-start.6
  7.2 0.0 copy-start.3
  7.2 4.2 copy.101
  11.5 3.4 reshape.167
  14.9 6.6 %all-to-all-start.1 = ((bf16[16,2,5120]{2,1,0:T(2,128)(2,1)}), bf16[16,2,5120]{2,1,0:T(2,128)(2,1)}, u32[]{:S(2)}, u32[]{:S(2)}) async-start(bf16[16,2,5120]{2,1,0:T(2,128)(2,1)} %reshape.167), calls=%async_computation.1 | async-start | bytes 655360 | tf_op jit(solution)/shard_map/all_to_all | solution.py:47
  21.5 0.0 all-gather.2.cloned.1.call-start
  21.5 0.7 all-gather.2.cloned.1.call-update
  22.2 0.1 reshape.97
  22.3 0.6 gather_fusion
  22.9 0.1 slice.9
  23.0 0.1 convert_reduce_fusion
  23.1 0.1 select_reduce_fusion.1
  23.1 24.2 %copy.96 = bf16[2,16,25600]{1,0,2:T(2,128)(2,1)} copy(bf16[2,16,25600]{2,1,0:T(8,128)(2,1)} %param.13) | data formatting | bytes 3276800 | tf_op args[4]
  47.4 18.3 %reshape.165 = bf16[16,2,25600]{2,1,0:T(2,128)(2,1)} reshape(bf16[25600,2,16]{2,1,0:T(2,128)(2,1)} %bitcast.94) | data formatting | bytes 3276800
  65.7 0.1 broadcast_multiply_fusion
  65.8 0.0 all-to-all-done.1
  65.8 6.0 %all-to-all-start = ((bf16[16,2,25600]{2,1,0:T(2,128)(2,1)}), bf16[16,2,25600]{2,1,0:T(2,128)(2,1)}, u32[]{:S(2)}, u32[]{:S(2)}) async-start(bf16[16,2,25600]{2,1,0:T(2,128)(2,1)} %reshape.165), calls=%async_computation | async-start | bytes 3276800 | tf_op jit(solution)/shard_map/all_to_all | solution.py:48
  71.8 0.2 reduce-scatter.2.cloned.1.call-start
  72.0 0.1 iota_add_fusion
  72.1 0.1 add.97
  72.2 0.1 add.94
  72.3 0.1 slice.11
  72.4 2.4 copy.95
  74.9 17.9 %convolution_bitcast_fusion = f32[256,5120]{1,0:T(8,128)} fusion(bf16[2,256,1600]{1,2,0:T(8,128)(2,1)S(1)} %broadcast_multiply_fusion, bf16[2,1600,5120]{2,1,0:T(8,128)(2,1)} %param.11), kind=kOutput, calls=%fused_computation.12 | convolution fusion | flops 8388608000 | bytes 39649280 | tf_op jit(solution)/shard_map/ptf,pfd->td/dot_general | solution.py:72
  92.8 8.5 %reshape.168 = bf16[5120,2,16]{2,1,0:T(2,128)(2,1)S(1)} reshape(bf16[16,2,5120]{2,1,0:T(2,128)(2,1)} %all-to-all-done.1) | data formatting | bytes 655360
  101.3 1.6 copy.102
  102.9 0.4 copy.103
  103.3 1.6 gather_fusion.3
  104.9 0.1 copy_select_fusion.1
  105.0 2.6 gather_fusion.4
  107.7 1.8 all-to-all-done
  109.5 14.8 %reshape.166 = bf16[25600,2,16]{2,1,0:T(2,128)(2,1)} reshape(bf16[16,2,25600]{2,1,0:T(2,128)(2,1)} %all-to-all-done) | data formatting | bytes 3276800
  124.3 28.1 %copy.97 = bf16[2,16,16,1600]{3,1,2,0:T(8,128)(2,1)S(1)} copy(bf16[2,16,16,1600]{1,0,3,2:T(2,128)(2,1)} %bitcast.93) | data formatting | bytes 3276800 | tf_op jit(solution)/shard_map/all_to_all | solution.py:48
  152.4 3.0 copy.98
  155.4 5.6 %gather_fusion.1 = bf16[256,2,1600]{2,1,0:T(2,128)(2,1)S(1)} fusion(bf16[2,256,1600]{2,0,1:T(2,128)(2,1)} %copy.98, s32[1024]{0:T(1024)S(1)} %pad_clamp_fusion.1), kind=kCustom, calls=%fused_computation.1 | custom fusion | bytes 3277824 | tf_op jit(solution)/shard_map/jit(_take)/gather | solution.py:51
  161.0 0.3 copy_select_fusion
  161.4 7.3 %gather_fusion.2 = bf16[32,2,64,1600]{3,2,1,0:T(8,128)(2,1)} fusion(bf16[2,4,64,1600]{3,2,1,0:T(8,128)(2,1)S(1)} %copy_select_fusion, s32[1024]{0:T(1024)S(1)} %pad_clamp_fusion), kind=kCustom, calls=%fused_computation.2 | custom fusion | bytes 26214528 | tf_op jit(solution)/shard_map/jit(_take)/gather | solution.py:54
  168.7 7.1 %fusion.2 = f32[2,32,8,64]{3,2,1,0:T(8,128)S(1)} fusion(bf16[2,256,1600]{2,1,0:T(8,128)(2,1)S(1)} %copy-done.1, bf16[32,2,64,1600]{3,2,1,0:T(8,128)(2,1)} %gather_fusion.2, pred[32]{0:T(512)(128)(4,1)S(1)} %compare_and_fusion.1), kind=kOutput, calls=%fused_computation.9 | convolution fusion | flops 111411200 | bytes 14876704 | tf_op jit(solution)/shard_map/pnbf,pnrf->pnbr/dot_general | solution.py:62
  175.8 3.7 convolution_bitcast_fusion.2
  179.5 49.4 %all-reduce.2 = (bf16[2,32,8,64]{3,2,1,0:T(8,128)(2,1)S(1)}, bf16[2,32,8,64]{3,2,0,1:T(8,128)(2,1)S(1)}) all-reduce(f32[2,32,8,64]{3,2,1,0:T(8,128)S(1)} %fusion.2, f32[2,32,8,64]{3,2,0,1:T(8,128)S(1)} %convolution_bitcast_fusion.2), channel_id=1, replica_groups=mesh['parts'=2,'tp'=16] {'tp'}, use_global_device_ids=true, to_apply=%region_3.4 | all-reduce | flops 65536 | bytes 393216 | tf_op jit(solution)/shard_map/psum | solution.py:65
  228.9 2.7 fusion.28
  231.6 3.7 add.100
  235.3 0.0 reduce-scatter.2.cloned.1.call-update
  235.3 2.0 convolution_bitcast_fusion.1
  237.4 5.7 %fusion.16 = f32[2,4,64,320]{3,1,2,0:T(4,128)S(1)} fusion(f32[2,32,64,320]{3,2,0,1:T(8,128)S(1)} %convolution_bitcast_fusion.1, s32[32]{0:T(128)S(1)} %slice.11), kind=kOutput, calls=%fused_computation.25 | convolution fusion | flops 63078528 | bytes 5898368 | tf_op jit(solution)/shard_map/ns,pnrd->psrd/dot_general | solution.py:86
  243.1 0.1 copy.108
  243.1 0.6 copy.109
  243.7 1.1 broadcast_in_dim.96
  244.8 28.8 %scatter_fusion = f32[2,256,320]{2,0,1:T(2,128)} fusion(f32[2,256,320]{2,0,1:T(2,128)} %broadcast_in_dim.96, s32[256]{0:T(256)S(1)} %bitcast.105, f32[256,2,320]{2,1,0:T(2,128)S(1)} %copy.109), kind=kCustom, calls=%fused_computation.5 | custom fusion | bytes 1967104 | tf_op jit(solution)/shard_map/scatter | solution.py:93
  273.7 21.2 %all-to-all-start.2 = ((f32[2,256,320]{2,0,1:T(2,128)}), f32[2,256,320]{2,0,1:T(2,128)}, u32[]{:S(2)}, u32[]{:S(2)}) async-start(f32[2,256,320]{2,0,1:T(2,128)} %scatter_fusion), calls=%async_computation.3 | async-start | bytes 1572864 | tf_op jit(solution)/shard_map/all_to_all | solution.py:101
  294.8 11.0 %fusion.10 = f32[2,32,64,1600]{3,2,1,0:T(8,128)} fusion(bf16[2,256,1600]{2,1,0:T(8,128)(2,1)S(1)} %copy-done.1, bf16[2,32,8,64]{3,2,0,1:T(8,128)(2,1)S(1)} %get-tuple-element.6), kind=kOutput, calls=%fused_computation.20 | convolution fusion | flops 104857600 | bytes 27918336 | tf_op jit(solution)/shard_map/pnbr,pnbf->pnrf/dot_general | solution.py:83
  305.9 32.4 %multiply_bitcast_fusion = f32[2,4,64,1600]{3,1,2,0:T(4,128)S(1)} fusion(f32[2,32,64,1600]{3,2,1,0:T(8,128)} %fusion.10, s32[32]{0:T(128)S(1)} %slice.11), kind=kOutput, calls=%fused_computation.15 | convolution fusion | flops 315392128 | bytes 29491328 | tf_op jit(solution)/shard_map/ns,pnrf->psrf/dot_general | solution.py:89
  338.3 0.2 copy.113
  338.5 2.6 copy.114
  341.2 2.6 broadcast_in_dim.97
  343.8 29.5 %scatter_fusion.1 = f32[2,256,1600]{2,0,1:T(2,128)} fusion(f32[2,256,1600]{2,0,1:T(2,128)} %broadcast_in_dim.97, s32[256]{0:T(256)S(1)} %bitcast.106, f32[256,2,1600]{2,1,0:T(2,128)S(1)} %copy.114), kind=kCustom, calls=%fused_computation.6 | custom fusion | bytes 9831424 | tf_op jit(solution)/shard_map/scatter | solution.py:97
  373.3 0.0 all-to-all-done.2
  373.3 6.1 %all-to-all-start.3 = ((f32[2,256,1600]{2,0,1:T(2,128)}), f32[2,256,1600]{2,0,1:T(2,128)S(1)}, u32[]{:S(2)}, u32[]{:S(2)}) async-start(f32[2,256,1600]{2,0,1:T(2,128)} %scatter_fusion.1), calls=%async_computation.4 | async-start | bytes 6815744 | tf_op jit(solution)/shard_map/all_to_all | solution.py:102
  379.3 2.5 copy.110
  381.8 2.2 all_to_all.63
  384.0 70.8 %all-to-all-done.3 = f32[2,256,1600]{2,0,1:T(2,128)S(1)} async-done(((f32[2,256,1600]{2,0,1:T(2,128)}), f32[2,256,1600]{2,0,1:T(2,128)S(1)}, u32[]{:S(2)}, u32[]{:S(2)}) %all-to-all-start.3) | async-done | bytes 3276832 | tf_op jit(solution)/shard_map/all_to_all | solution.py:102
  454.8 1.7 copy-done
  456.6 3.9 copy.115
  460.5 2.7 all_to_all.67
  (23 shorter events, 0.1 us)
Async XLA Ops:
  7.2 15.0 %copy-start.6 = (s32[4]{0:T(128)S(1)}, s32[4]{0:T(128)}, u32[]{:S(2)}) copy-start(s32[4]{0:T(128)} %param.14) | copy-start | bytes 52
  7.2 15.0 %copy-start.3 = (s32[16]{0:T(128)S(1)}, s32[16]{0:T(128)}, u32[]{:S(2)}) copy-start(s32[16]{0:T(128)} %param.15) | copy-start | bytes 196
  7.2 15.7 %copy-start.4 = (s32[5]{0:T(128)S(1)}, s32[5]{0:T(128)}, u32[]{:S(2)}) copy-start(s32[5]{0:T(128)} %param.16) | copy-start | bytes 64
  7.2 15.9 %copy-start.5 = (s32[4]{0:T(128)S(1)}, s32[4]{0:T(128)}, u32[]{:S(2)}) copy-start(s32[4]{0:T(128)} %param.17) | copy-start | bytes 52
  14.9 50.9 %all-to-all-start.1 = ((bf16[16,2,5120]{2,1,0:T(2,128)(2,1)}), bf16[16,2,5120]{2,1,0:T(2,128)(2,1)}, u32[]{:S(2)}, u32[]{:S(2)}) async-start(bf16[16,2,5120]{2,1,0:T(2,128)(2,1)} %reshape.167), calls=%async_computation.1 | async-start | bytes 655360 | tf_op jit(solution)/shard_map/all_to_all | solution.py:47
  21.5 154.3 %all-gather.2.cloned.1.call-start = ((), (), s32[]{:S(2)}) async-start(), calls=%async_computation.6 | async-start | bytes 2785280 | tf_op jit(solution)/shard_map/all_gather | solution.py:55
  47.4 18.3 %copy-start.2 = (bf16[2,256,1600]{1,2,0:T(8,128)(2,1)S(1)}, bf16[2,256,1600]{1,2,0:T(8,128)(2,1)}, u32[]{:S(2)}) copy-start(bf16[2,256,1600]{1,2,0:T(8,128)(2,1)} %param.10) | copy-start | bytes 4915204
  65.8 43.7 %all-to-all-start = ((bf16[16,2,25600]{2,1,0:T(2,128)(2,1)}), bf16[16,2,25600]{2,1,0:T(2,128)(2,1)}, u32[]{:S(2)}, u32[]{:S(2)}) async-start(bf16[16,2,25600]{2,1,0:T(2,128)(2,1)} %reshape.165), calls=%async_computation | async-start | bytes 3276800 | tf_op jit(solution)/shard_map/all_to_all | solution.py:48
  71.8 391.4 %reduce-scatter.2.cloned.1.call-start = ((), (), s32[]{:S(2)}) async-start(), calls=%async_computation.5 | async-start | bytes 5570560 | tf_op jit(solution)/shard_map/reduce_scatter | solution.py:78
  161.3 7.3 %copy-start.1 = (bf16[2,256,1600]{2,1,0:T(8,128)(2,1)S(1)}, bf16[2,256,1600]{2,1,0:T(8,128)(2,1)}, u32[]{:S(2)}) copy-start(bf16[2,256,1600]{2,1,0:T(8,128)(2,1)} %copy.95) | copy-start | bytes 4915204
  273.7 99.6 %all-to-all-start.2 = ((f32[2,256,320]{2,0,1:T(2,128)}), f32[2,256,320]{2,0,1:T(2,128)}, u32[]{:S(2)}, u32[]{:S(2)}) async-start(f32[2,256,320]{2,0,1:T(2,128)} %scatter_fusion), calls=%async_computation.3 | async-start | bytes 1572864 | tf_op jit(solution)/shard_map/all_to_all | solution.py:101
  373.3 81.6 %all-to-all-start.3 = ((f32[2,256,1600]{2,0,1:T(2,128)}), f32[2,256,1600]{2,0,1:T(2,128)S(1)}, u32[]{:S(2)}, u32[]{:S(2)}) async-start(f32[2,256,1600]{2,0,1:T(2,128)} %scatter_fusion.1), calls=%async_computation.4 | async-start | bytes 6815744 | tf_op jit(solution)/shard_map/all_to_all | solution.py:102
  454.8 1.7 copy-start
Sparse Core Ops, SparseCore 0:
  24.6 43.1 all-gather.1
  235.5 103.2 reduce-scatter.1
where the time goes:
time: 480 us; the launch traced here: 470 us
  local copies, waits for them, and re-layouts  209 us (44%)
  matrix products  82.6 us (17%)
  waiting for transfers between devices  73.4 us (15%)
  blocking collectives  49.4 us (10%)
  starting transfers between devices  40 us (8%)
  between operations  14.5 us (3%)
    unnamed x20, local copies, waits for them, and re-layouts  75.3 us
    all_to_all x1, waiting for transfers between devices, shards(): lax.all_to_all(local_second, 'tp', split_axis=1, concat_axis=2, tiled=True)  70.8 us
    psum x1, blocking collectives, shards(): rank_projection, rank_backward = lax.psum((low_part, back_part), 'tp')  49.4 us
    dot_general x1, matrix products, shards(): jnp.einsum('ns,pnrf->psrf', block_onehot, second_terms, precision=lax.Pre...  32.4 us
    all_to_all x2, local copies, waits for them, and re-layouts, shards(): lax.all_to_all(adapter_second, 'tp', split_axis=2, concat_axis=1, tiled=T...  31.1 us
    scatter x1, local copies, waits for them, and re-layouts, shards(): local_second.at[:, rows_flat]  29.5 us
    scatter x1, local copies, waits for them, and re-layouts, shards(): local_first.at[:, rows_flat]  28.8 us
    all_to_all x1, starting transfers between devices, shards(): lax.all_to_all(local_first, 'tp', split_axis=1, concat_axis=2, tiled=True)  21.2 us
  transfers between devices with their start and end apart: 6, of which 2 were waited for; matrix products, arithmetic and copies ran while one was open for 57% of the time, Pallas kernels for 0%

commit v1 on v0

v1 whole, which is shorter than its diff:
```python
import functools

import jax
import jax.numpy as jnp
from jax import lax
from jax.experimental import pallas as pl
from jax.experimental.pallas import tpu as pltpu
from jax.sharding import PartitionSpec as P

R = 64
SPLIT = 4
adapter_scale = 0.5
PARAMS = pltpu.CompilerParams(vmem_limit_bytes=48 * 1024 * 1024)
f32 = jnp.float32
bf16 = jnp.bfloat16


def pack_kernel(tp, hidden, width, second_ref, first_ref, inputs_ref, out_ref):
    piece, tok, half = first_ref.shape[1], inputs_ref.shape[0], width // 2
    at = hidden + width
    for d in range(tp):
        for p in range(2):
            rows = slice(p * piece, (p + 1) * piece)
            out_ref[d, rows, :hidden] = second_ref[p, :, d * hidden : (d + 1) * hidden]
            out_ref[d, rows, hidden:at] = first_ref[p, :, d * width : (d + 1) * width]
            start = d * width + p * half
            out_ref[d, p * piece : p * piece + tok, at:] = inputs_ref[:, start : start + half]


def contract(a, b, dims, precision=None):
    return lax.dot_general(a, b, (dims, ((), ())), precision=precision, preferred_element_type=f32)


def project_kernel(
    tp, hidden, width, piece, tok, got_ref, grads_ref, live_ref, match_ref, pick_ref, out_ref, cols_ref, x_ref
):
    half, at = width // 2, hidden + width
    for d in range(tp):
        for p in range(2):
            x_ref[d * tok : (d + 1) * tok, p * half : (p + 1) * half] = got_ref[
                d, p * piece : p * piece + tok, at:
            ].astype(f32)
    x = x_ref[...].astype(bf16)
    cols_ref[...] = x
    match = match_ref[...]
    pick = pick_ref[...]
    live = live_ref[...]
    for p in range(2):
        rows = slice(p * piece, (p + 1) * piece)
        first = got_ref[:, rows, hidden:at].reshape(tp * piece, width)
        second = got_ref[:, rows, :hidden].reshape(tp * piece, hidden)
        low = contract(x, first, ((1,), (1,)))
        back = contract(grads_ref[p] * live, second, ((1,), (1,)))
        for k, value in ((p, low), (2 + p, back)):
            kept = jnp.where(match > 0, value, 0.0)
            out_ref[:, k * R : (k + 1) * R] = contract(
                kept, pick, ((1,), (0,)), precision=lax.Precision.HIGHEST
            )


def gradient_kernel(
    tp, hidden, width, piece, tok, got_ref, grads_ref, live_ref, match_ref, pick_ref, cols_ref, rank_ref, out_ref, a_ref
):
    half, at = width // 2, hidden + width
    match = match_ref[...]
    pick = pick_ref[...].astype(bf16)
    live = live_ref[...]
    x = cols_ref[...]
    total = None
    for p in range(2):
        rows = slice(p * piece, (p + 1) * piece)

        def spread(k):
            wide = contract(rank_ref[:, k * R : (k + 1) * R], pick, ((1,), (1,)))
            return jnp.where(match > 0, wide, 0.0).astype(bf16)

        low, back = spread(p), spread(2 + p)
        first = got_ref[:, rows, hidden:at].reshape(tp * piece, width)
        term = contract(back, first, ((1,), (0,)))
        total = term if total is None else total + term
        first_gradient = adapter_scale * contract(back, x, ((0,), (0,)))
        out_ref[:, rows, hidden:at] = first_gradient.astype(bf16).reshape(tp, piece, width)
        second_gradient = adapter_scale * contract(low, grads_ref[p] * live, ((0,), (0,)))
        out_ref[:, rows, :hidden] = second_gradient.astype(bf16).reshape(tp, piece, hidden)
    a_ref[...] = adapter_scale * total
    for d in range(tp):
        for p in range(2):
            out_ref[d, p * piece : p * piece + tok, at:] = a_ref[
                d * tok : (d + 1) * tok, p * half : (p + 1) * half
            ].astype(bf16)


def unpack_kernel(tp, hidden, width, got_ref, base_ref, grads_ref, first_ref, second_ref):
    piece, tok, half = first_ref.shape[1], base_ref.shape[0], width // 2
    at = hidden + width
    for d in range(tp):
        for p in range(2):
            rows = slice(p * piece, (p + 1) * piece)
            second_ref[p, :, d * hidden : (d + 1) * hidden] = got_ref[d, rows, :hidden].astype(f32)
            first_ref[p, :, d * width : (d + 1) * width] = got_ref[d, rows, hidden:at].astype(f32)
            cut = slice(d * width + p * half, d * width + (p + 1) * half)
            grads_ref[:, cut] = base_ref[:, cut] + got_ref[d, p * piece : p * piece + tok, at:].astype(f32)


def shards(
    inputs,
    out_grads,
    frozen_weights,
    adapter_first,
    adapter_second,
    group_jobs,
    owner_map,
    segment_offsets,
    segment_lengths,
):
    tp = lax.axis_size("tp")
    job_count = group_jobs.shape[0]
    tokens, hidden = out_grads.shape[1:]
    tok, model = inputs.shape
    width = model // tp
    piece = adapter_first.shape[1]
    total_rows = tp * piece
    wide = hidden + width + width // 2
    sizes = (tp, hidden, width)

    packed = pl.pallas_call(
        functools.partial(pack_kernel, *sizes),
        out_shape=jax.ShapeDtypeStruct((tp, 2 * piece, wide), bf16),
        compiler_params=PARAMS,
    )(adapter_second, adapter_first, inputs)
    got = lax.all_to_all(packed, "tp", split_axis=0, concat_axis=0, tiled=True)

    positions = jnp.arange(tokens, dtype=jnp.int32)
    slot_ids = jnp.arange(job_count, dtype=jnp.int32)
    slot_of = jnp.sum((positions[:, None] >= segment_offsets[1:job_count][None, :]).astype(jnp.int32), axis=1)
    onehot = slot_of[:, None] == slot_ids[None, :]
    starts = jnp.sum(jnp.where(onehot, segment_offsets[:job_count][None, :], 0), axis=1)
    spans = jnp.sum(jnp.where(onehot, segment_lengths[None, :], 0), axis=1)
    live = (positions - starts < spans).astype(out_grads.dtype)[:, None]
    row = jnp.arange(total_rows, dtype=jnp.int32)
    entries = jnp.arange(tp, dtype=jnp.int32)
    entry = jnp.sum(jnp.where(owner_map[None, :] == (row // piece)[:, None], entries[None, :], 0), axis=1)
    row_slot = jnp.sum(
        jnp.where(group_jobs[None, :] == (entry // SPLIT)[:, None], slot_ids[None, :], 0), axis=1
    )
    rank = (entry % SPLIT) * piece + row % piece
    match = (slot_of[:, None] == row_slot[None, :]).astype(f32)
    pick = (rank[:, None] == jnp.arange(R, dtype=jnp.int32)[None, :]).astype(f32)

    masked = out_grads * live[None]
    frozen_product = jnp.einsum("ptf,pfd->td", masked, frozen_weights, preferred_element_type=f32)
    frozen_rows = lax.psum_scatter(frozen_product, "tp", scatter_dimension=0, tiled=True)

    parts, columns = pl.pallas_call(
        functools.partial(project_kernel, *sizes, piece, tok),
        out_shape=(
            jax.ShapeDtypeStruct((tokens, 4 * R), f32),
            jax.ShapeDtypeStruct((tokens, width), bf16),
        ),
        scratch_shapes=[pltpu.VMEM((tokens, width), f32)],
        compiler_params=PARAMS,
    )(got, out_grads, live, match, pick)
    swapped = lax.all_to_all(parts.reshape(tp, tok, 4 * R), "tp", split_axis=0, concat_axis=0, tiled=True)
    own_rank = jnp.sum(swapped, axis=0).astype(bf16)
    rank_values = lax.all_gather(own_rank, "tp", axis=0, tiled=True)

    outgoing = pl.pallas_call(
        functools.partial(gradient_kernel, *sizes, piece, tok),
        out_shape=jax.ShapeDtypeStruct((tp, 2 * piece, wide), bf16),
        scratch_shapes=[pltpu.VMEM((tokens, width), f32)],
        compiler_params=PARAMS,
    )(got, out_grads, live, match, pick, columns, rank_values)
    returned = lax.all_to_all(outgoing, "tp", split_axis=0, concat_axis=0, tiled=True)
    return pl.pallas_call(
        functools.partial(unpack_kernel, *sizes),
        out_shape=(
            jax.ShapeDtypeStruct((tok, model), f32),
            jax.ShapeDtypeStruct((2, piece, model), f32),
            jax.ShapeDtypeStruct((2, piece, tp * hidden), f32),
        ),
        compiler_params=PARAMS,
    )(returned, frozen_rows)


def solution(mesh):
    return jax.shard_map(
        shards,
        mesh=mesh,
        in_specs=(
            P(("parts", "tp"), None),
            P(None, "parts", "tp"),
            P(None, "tp", None),
            P(None, ("parts", "tp"), None),
            P(None, ("parts", "tp"), None),
            P("parts"),
            P("parts"),
            P("parts"),
            P("parts"),
        ),
        out_specs=(
            P(("parts", "tp"), None),
            P(None, ("parts", "tp"), None),
            P(None, ("parts", "tp"), None),
        ),
        check_vma=False,
    )
```

time: 480 us -> 187 us (0.39); the launches traced: 470 us -> 186 us
  local copies, waits for them, and re-layouts: 209 us -> 13.9 us
  matrix products: 82.6 us -> 16.9 us
  starting transfers between devices: 40 us -> 16.8 us
  blocking collectives: 49.4 us -> 36.2 us
  Pallas kernels: 0 us -> 7.82 us
  waiting for transfers between devices: 73.4 us -> 79.9 us
    dot_general x7 -> x0, matrix products: 64.7 us -> none  [the longest x1 32.4 us: shards(): jnp.einsum('ns,pnrf->psrf', block_onehot, second_terms, precision=lax.Pre...]
    unnamed x20 -> x27, local copies, waits for them, and re-layouts: 75.3 us -> 13.5 us
    scatter x2 -> x0, local copies, waits for them, and re-layouts: 58.3 us -> none  [the longest x1 29.5 us: shards(): local_second.at[:, rows_flat]]
    psum x1 -> x0, blocking collectives: 49.4 us -> none  [shards(): rank_projection, rank_backward = lax.psum((low_part, back_part), 'tp')]
    all_to_all x8 -> x0, local copies, waits for them, and re-layouts: 44.4 us -> none  [the longest x2 31.1 us: shards(): lax.all_to_all(adapter_second, 'tp', split_axis=2, concat_axis=1, tiled=T...]
    all_to_all x4 -> x2, starting transfers between devices: 39.8 us -> 16.7 us  [the longest x1 10 us: shards(): lax.all_to_all(outgoing, 'tp', split_axis=0, concat_axis=0, tiled=True)]
    all_to_all x0 -> x1, blocking collectives: none -> 20.4 us  [shards(): lax.all_to_all(parts.reshape(tp, tok, 4 * R), 'tp', split_axis=0, concat_...]
    gather x5 -> x0, local copies, waits for them, and re-layouts: 17.7 us -> none  [the longest x1 7.31 us: shards(): block_second = jnp.take(slot_second, block_slot, axis=1)]
  transfers between devices with their start and end apart: 6 -> 3, of which waited for: 2 -> 2; matrix products, arithmetic and copies ran while one was open for 57% -> 12% of each run, Pallas kernels for 0% -> 3%
where the time goes in v1:
time: 187 us; the launch traced here: 186 us
  waiting for transfers between devices  79.9 us (43%)
  blocking collectives  36.2 us (19%)
  matrix products  16.9 us (9%)
  starting transfers between devices  16.8 us (9%)
  between operations  14.2 us (8%)
  local copies, waits for them, and re-layouts  13.9 us (7%)
  Pallas kernels  7.82 us (4%)
    all_to_all x1, waiting for transfers between devices, shards(): lax.all_to_all(outgoing, 'tp', split_axis=0, concat_axis=0, tiled=True)  50.2 us
    all_to_all x1, waiting for transfers between devices, shards(): got = lax.all_to_all(packed, 'tp', split_axis=0, concat_axis=0, tiled=True)  29.6 us
    all_to_all x1, blocking collectives, shards(): lax.all_to_all(parts.reshape(tp, tok, 4 * R), 'tp', split_axis=0, concat_...  20.4 us
    dot_general x1, matrix products, shards(): jnp.einsum('ptf,pfd->td', masked, frozen_weights, preferred_element_type=...  16.9 us
    all_gather x1, blocking collectives, shards(): rank_values = lax.all_gather(own_rank, 'tp', axis=0, tiled=True)  15.8 us
    unnamed x27, local copies, waits for them, and re-layouts  13.5 us
    all_to_all x1, starting transfers between devices, shards(): lax.all_to_all(outgoing, 'tp', split_axis=0, concat_axis=0, tiled=True)  10 us
    all_to_all x1, starting transfers between devices, shards(): got = lax.all_to_all(packed, 'tp', split_axis=0, concat_axis=0, tiled=True)  6.69 us
  transfers between devices with their start and end apart: 3, of which 2 were waited for; matrix products, arithmetic and copies ran while one was open for 12% of the time, Pallas kernels for 3%

profile of v1, /device:TPU:11, one launch (start us, length us, event | category | flops | bytes accessed | tf_op | source)
XLA Modules:
  0.0 186.3 jit_solution(14252991719965341509)
XLA Ops:
  7.2 0.0 copy-start.5
  7.2 1.4 copy-done.5
  8.6 0.0 copy-start.6
  8.6 1.0 copy-done.6
  9.6 0.0 copy-start.8
  9.6 0.9 copy-done.8
  10.5 0.4 shard_map.112
  10.9 0.0 copy-start.3
  10.9 1.4 copy-done.3
  12.3 0.0 copy-start.12
  12.3 0.0 copy-start.11
  12.3 6.7 %all-to-all-start = ((bf16[16,32,2080]{2,1,0:T(8,128)(2,1)}), bf16[16,32,2080]{2,1,0:T(8,128)(2,1)S(1)}, u32[]{:S(2)}, u32[]{:S(2)}) async-start(bf16[16,32,2080]{2,1,0:T(8,128)(2,1)} %copy-done.3), calls=%async_computation | async-start | bytes 4456448 | tf_op jit(solution)/shard_map/all_to_all | solution.py:131
  19.0 0.0 reduce-scatter.2.cloned.1.call-start
  19.0 0.0 copy-done.12
  19.0 0.1 slice.6
  19.1 0.1 convert_reduce_fusion
  19.2 0.0 copy-done.11
  19.2 0.1 select_reduce_fusion.2
  19.3 16.9 %convolution_bitcast_fusion = f32[256,5120]{1,0:T(8,128)} fusion(bf16[2,1600,5120]{2,1,0:T(8,128)(2,1)} %param.11, bf16[2,256,1600]{1,2,0:T(8,128)(2,1)} %param.10, bf16[256]{0:T(256)(128)(2,1)S(1)} %compare_convert_fusion.2), kind=kOutput, calls=%fused_computation | convolution fusion | flops 8389427200 | bytes 39649792 | tf_op jit(solution)/shard_map/ptf,pfd->td/dot_general | solution.py:151
  36.2 0.0 reduce-scatter.2.cloned.1.call-update
  36.2 0.0 copy-start.9
  36.2 0.0 copy-start.10
  36.3 3.6 %copy.25.grads_ref = bf16[2,256,1600]{2,1,0:T(8,128)(2,1)} copy(bf16[2,256,1600]{1,2,0:T(8,128)(2,1)} %param.10) | data formatting | bytes 3276800 | tf_op args[1]
  39.8 0.1 copy.22
  40.0 0.1 copy.23
  40.1 0.0 copy-done.9
  40.2 0.1 select_reduce_fusion
  40.3 0.0 copy-done.10
  40.3 0.1 select_reduce_fusion.1
  40.4 0.1 fusion.2.pick_ref
  40.5 0.1 compare_convert_fusion.match_ref
  40.6 29.6 %all-to-all-done.got_ref = bf16[16,32,2080]{2,1,0:T(8,128)(2,1)S(1)} async-done(((bf16[16,32,2080]{2,1,0:T(8,128)(2,1)}), bf16[16,32,2080]{2,1,0:T(8,128)(2,1)S(1)}, u32[]{:S(2)}, u32[]{:S(2)}) %all-to-all-start) | async-done | bytes 2129952 | tf_op jit(solution)/shard_map/all_to_all | solution.py:131
  70.2 0.0 copy-start.1
  70.2 1.5 copy-done.1
  71.7 0.0 copy-start
  71.7 1.9 %shard_map.113 = (f32[256,256]{1,0:T(8,128)S(1)}, bf16[256,320]{1,0:T(8,128)(2,1)S(1)}) custom-call(bf16[16,32,2080]{2,1,0:T(8,128)(2,1)S(1)} %all-to-all-done.got_ref, bf16[2,256,1600]{2,1,0:T(8,128)(2,1)S(1)} %copy-done.1, bf16[256,1]{1,0:T(8,128)(2,1)S(1)} %compare_convert_fusion.1.live_ref, f32[256,256]{1,0:T(8,128)S(1)} %compare_convert_fusion.match_ref, ...), custom_call_target="tpu_custom_call" | custom-call | tf_op jit(solution)/shard_map/pallas_call | solution.py:154
  73.6 20.4 %all_to_all.15 = f32[16,16,256]{2,1,0:T(8,128)S(1)} all-to-all(f32[16,16,256]{2,1,0:T(8,128)S(1)} %bitcast.7), channel_id=1, replica_groups=mesh['parts'=2,'tp'=16] {'tp'}, dimensions={0} | all-to-all | bytes 524288 | tf_op jit(solution)/shard_map/all_to_all | solution.py:163
  94.0 0.0 copy-done
  94.1 15.8 %all_gather.3.rank_ref = bf16[256,256]{1,0:T(8,128)(2,1)S(1)} all-gather(bf16[16,256]{1,0:T(8,128)(2,1)S(1)} %reduce_sum.65), channel_id=1, replica_groups=mesh['parts'=2,'tp'=16] {'tp'}, dimensions={0}, use_global_device_ids=true | all-gather | bytes 139264 | tf_op jit(solution)/shard_map/all_gather | solution.py:165
  109.9 0.0 copy-start.2
  109.9 1.5 copy-done.2
  111.3 3.1 %shard_map.114 = bf16[16,32,2080]{2,1,0:T(8,128)(2,1)S(1)} custom-call(bf16[16,32,2080]{2,1,0:T(8,128)(2,1)} %copy-done, bf16[2,256,1600]{2,1,0:T(8,128)(2,1)S(1)} %copy-done.2, bf16[256,1]{1,0:T(8,128)(2,1)S(1)} %compare_convert_fusion.1.live_ref, f32[256,256]{1,0:T(8,128)S(1)} %compare_convert_fusion.match_ref, f32[256,64]{1,0:T(8,128)S(1)} %fusion.2.pick_ref, ...), custom_call_target="tpu_custom_call" | custom-call | tf_op jit(solution)/shard_map/pallas_call | solution.py:167
  114.4 0.0 copy-start.4
  114.4 1.4 copy-done.4
  115.8 10.0 %all-to-all-start.2 = ((bf16[16,32,2080]{2,1,0:T(8,128)(2,1)}), bf16[16,32,2080]{2,1,0:T(8,128)(2,1)S(1)}, u32[]{:S(2)}, u32[]{:S(2)}) async-start(bf16[16,32,2080]{2,1,0:T(8,128)(2,1)} %copy-done.4), calls=%async_computation.2 | async-start | bytes 4456448 | tf_op jit(solution)/shard_map/all_to_all | solution.py:173
  125.8 0.0 reduce-scatter.2.cloned.1.call-done.base_ref
  125.8 50.2 %all-to-all-done.2.got_ref = bf16[16,32,2080]{2,1,0:T(8,128)(2,1)S(1)} async-done(((bf16[16,32,2080]{2,1,0:T(8,128)(2,1)}), bf16[16,32,2080]{2,1,0:T(8,128)(2,1)S(1)}, u32[]{:S(2)}, u32[]{:S(2)}) %all-to-all-start.2) | async-done | bytes 2129952 | tf_op jit(solution)/shard_map/all_to_all | solution.py:173
  176.1 0.0 copy-start.7
  176.1 1.0 copy-done.7
  177.0 2.4 %shard_map.115 = (f32[16,5120]{1,0:T(8,128)}, f32[2,16,5120]{2,1,0:T(8,128)}, f32[2,16,25600]{2,1,0:T(8,128)}) custom-call(bf16[16,32,2080]{2,1,0:T(8,128)(2,1)S(1)} %all-to-all-done.2.got_ref, f32[16,5120]{1,0:T(8,128)S(1)} %copy-done.7), custom_call_target="tpu_custom_call" | custom-call | tf_op jit(solution)/shard_map/pallas_call | solution.py:174
  (6 shorter events, 0.1 us)
Async XLA Ops:
  7.2 1.4 copy-start.5
  8.6 1.0 copy-start.6
  9.6 0.9 copy-start.8
  10.9 1.4 copy-start.3
  12.3 6.7 %copy-start.12 = (s32[5]{0:T(128)S(1)}, s32[5]{0:T(128)}, u32[]{:S(2)}) copy-start(s32[5]{0:T(128)} %param.16) | copy-start | bytes 64
  12.3 6.9 %copy-start.11 = (s32[4]{0:T(128)S(1)}, s32[4]{0:T(128)}, u32[]{:S(2)}) copy-start(s32[4]{0:T(128)} %param.17) | copy-start | bytes 52
  12.3 57.9 %all-to-all-start = ((bf16[16,32,2080]{2,1,0:T(8,128)(2,1)}), bf16[16,32,2080]{2,1,0:T(8,128)(2,1)S(1)}, u32[]{:S(2)}, u32[]{:S(2)}) async-start(bf16[16,32,2080]{2,1,0:T(8,128)(2,1)} %copy-done.3), calls=%async_computation | async-start | bytes 4456448 | tf_op jit(solution)/shard_map/all_to_all | solution.py:131
  19.0 106.8 %reduce-scatter.2.cloned.1.call-start = ((), (), s32[]{:S(2)}) async-start(), calls=%async_computation.4 | async-start | bytes 5570560 | tf_op jit(solution)/shard_map/reduce_scatter | solution.py:152
  36.2 3.9 %copy-start.9 = (s32[16]{0:T(128)S(1)}, s32[16]{0:T(128)}, u32[]{:S(2)}) copy-start(s32[16]{0:T(128)} %param.15) | copy-start | bytes 196
  36.2 4.0 %copy-start.10 = (s32[4]{0:T(128)S(1)}, s32[4]{0:T(128)}, u32[]{:S(2)}) copy-start(s32[4]{0:T(128)} %param.14) | copy-start | bytes 52
  70.2 1.5 copy-start.1
  71.7 22.4 %copy-start = (bf16[16,32,2080]{2,1,0:T(8,128)(2,1)}, bf16[16,32,2080]{2,1,0:T(8,128)(2,1)S(1)}, u32[]{:S(2)}) copy-start(bf16[16,32,2080]{2,1,0:T(8,128)(2,1)S(1)} %all-to-all-done.got_ref) | copy-start | bytes 6389764
  109.9 1.5 copy-start.2
  114.4 1.4 copy-start.4
  115.8 60.3 %all-to-all-start.2 = ((bf16[16,32,2080]{2,1,0:T(8,128)(2,1)}), bf16[16,32,2080]{2,1,0:T(8,128)(2,1)S(1)}, u32[]{:S(2)}, u32[]{:S(2)}) async-start(bf16[16,32,2080]{2,1,0:T(8,128)(2,1)} %copy-done.4), calls=%async_computation.2 | async-start | bytes 4456448 | tf_op jit(solution)/shard_map/all_to_all | solution.py:173
  176.1 1.0 copy-start.7
Sparse Core Ops, SparseCore 0:
  36.4 81.4 reduce-scatter.1

commit v2 on v1

--- a/solution.py
+++ b/solution.py
@@ -31,17 +31,29 @@
     return lax.dot_general(a, b, (dims, ((), ())), precision=precision, preferred_element_type=f32)
 
 
-def project_kernel(
-    tp, hidden, width, piece, tok, got_ref, grads_ref, live_ref, match_ref, pick_ref, out_ref, cols_ref, x_ref
+def middle_kernel(
+    tp, hidden, width, piece, tok, got_ref, grads_ref, live_ref, match_ref, pick_ref, out_ref,
+    x_ref, flat_ref, parts_ref, landed_ref, rank_ref, sent_parts, came_parts, sent_rank, came_rank,
 ):
     half, at = width // 2, hidden + width
+    me = lax.axis_index("tp")
+
+    barrier = pltpu.get_barrier_semaphore()
+
+    def greet(k, carry):
+        pl.semaphore_signal(
+            barrier, inc=1, device_id={"tp": lax.rem(me + k, tp)}, device_id_type=pl.DeviceIdType.MESH
+        )
+        return carry
+
+    lax.fori_loop(1, tp, greet, 0)
+
     for d in range(tp):
         for p in range(2):
             x_ref[d * tok : (d + 1) * tok, p * half : (p + 1) * half] = got_ref[
                 d, p * piece : p * piece + tok, at:
             ].astype(f32)
     x = x_ref[...].astype(bf16)
-    cols_ref[...] = x
     match = match_ref[...]
     pick = pick_ref[...]
     live = live_ref[...]
@@ -53,26 +65,69 @@
         back = contract(grads_ref[p] * live, second, ((1,), (1,)))
         for k, value in ((p, low), (2 + p, back)):
             kept = jnp.where(match > 0, value, 0.0)
-            out_ref[:, k * R : (k + 1) * R] = contract(
+            flat_ref[:, k * R : (k + 1) * R] = contract(
                 kept, pick, ((1,), (0,)), precision=lax.Precision.HIGHEST
             )
-
-
-def gradient_kernel(
-    tp, hidden, width, piece, tok, got_ref, grads_ref, live_ref, match_ref, pick_ref, cols_ref, rank_ref, out_ref, a_ref
-):
-    half, at = width // 2, hidden + width
-    match = match_ref[...]
-    pick = pick_ref[...].astype(bf16)
-    live = live_ref[...]
-    x = cols_ref[...]
+    for d in range(tp):
+        parts_ref[d] = flat_ref[d * tok : (d + 1) * tok, :]
+    landed_ref[me] = parts_ref[me]
+
+    def push(k, source, target, sent, came):
+        return pltpu.make_async_remote_copy(
+            src_ref=source,
+            dst_ref=target.at[me],
+            send_sem=sent.at[k],
+            recv_sem=came.at[me],
+            device_id={"tp": lax.rem(me + k, tp)},
+            device_id_type=pl.DeviceIdType.MESH,
+        )
+
+    def arrival(k, target, sent, came):
+        origin = lax.rem(me + k, tp)
+        return pltpu.make_async_remote_copy(
+            src_ref=target.at[origin],
+            dst_ref=target.at[origin],
+            send_sem=sent.at[k],
+            recv_sem=came.at[origin],
+            device_id={"tp": origin},
+            device_id_type=pl.DeviceIdType.MESH,
+        )
+
+    def each(body):
+        def step(k, carry):
+            body(k)
+            return carry
+
+        lax.fori_loop(1, tp, step, 0)
+
+    def parts_copy(k):
+        return push(k, parts_ref.at[lax.rem(me + k, tp)], landed_ref, sent_parts, came_parts)
+
+    def rank_copy(k):
+        return push(k, rank_ref.at[me], rank_ref, sent_rank, came_rank)
+
+    pl.semaphore_wait(barrier, tp - 1)
+    each(lambda k: parts_copy(k).start())
+    each(lambda k: arrival(k, landed_ref, sent_parts, came_parts).wait_recv())
+    own = landed_ref[0]
+    for d in range(1, tp):
+        own = own + landed_ref[d]
+    rank_ref[me] = own
+    each(lambda k: rank_copy(k).start())
+    each(lambda k: parts_copy(k).wait_send())
+    each(lambda k: arrival(k, rank_ref, sent_rank, came_rank).wait_recv())
+    each(lambda k: rank_copy(k).wait_send())
+    for d in range(tp):
+        flat_ref[d * tok : (d + 1) * tok, :] = rank_ref[d]
+
+    short_pick = pick.astype(bf16)
     total = None
     for p in range(2):
         rows = slice(p * piece, (p + 1) * piece)
 
         def spread(k):
-            wide = contract(rank_ref[:, k * R : (k + 1) * R], pick, ((1,), (1,)))
-            return jnp.where(match > 0, wide, 0.0).astype(bf16)
+            values = flat_ref[:, k * R : (k + 1) * R].astype(bf16)
+            return jnp.where(match > 0, contract(values, short_pick, ((1,), (1,))), 0.0).astype(bf16)
 
         low, back = spread(p), spread(2 + p)
         first = got_ref[:, rows, hidden:at].reshape(tp * piece, width)
@@ -82,10 +137,10 @@
         out_ref[:, rows, hidden:at] = first_gradient.astype(bf16).reshape(tp, piece, width)
         second_gradient = adapter_scale * contract(low, grads_ref[p] * live, ((0,), (0,)))
         out_ref[:, rows, :hidden] = second_gradient.astype(bf16).reshape(tp, piece, hidden)
-    a_ref[...] = adapter_scale * total
-    for d in range(tp):
-        for p in range(2):
-            out_ref[d, p * piece : p * piece + tok, at:] = a_ref[
+    x_ref[...] = adapter_scale * total
+    for d in range(tp):
+        for p in range(2):
+            out_ref[d, p * piece : p * piece + tok, at:] = x_ref[
                 d * tok : (d + 1) * tok, p * half : (p + 1) * half
             ].astype(bf16)
 
@@ -151,25 +206,24 @@
     frozen_product = jnp.einsum("ptf,pfd->td", masked, frozen_weights, preferred_element_type=f32)
     frozen_rows = lax.psum_scatter(frozen_product, "tp", scatter_dimension=0, tiled=True)
 
-    parts, columns = pl.pallas_call(
-        functools.partial(project_kernel, *sizes, piece, tok),
-        out_shape=(
-            jax.ShapeDtypeStruct((tokens, 4 * R), f32),
-            jax.ShapeDtypeStruct((tokens, width), bf16),
-        ),
-        scratch_shapes=[pltpu.VMEM((tokens, width), f32)],
-        compiler_params=PARAMS,
+    outgoing = pl.pallas_call(
+        functools.partial(middle_kernel, *sizes, piece, tok),
+        out_shape=jax.ShapeDtypeStruct((tp, 2 * piece, wide), bf16),
+        scratch_shapes=[
+            pltpu.VMEM((tokens, width), f32),
+            pltpu.VMEM((tokens, 4 * R), f32),
+            pltpu.VMEM((tp, tok, 4 * R), f32),
+            pltpu.VMEM((tp, tok, 4 * R), f32),
+            pltpu.VMEM((tp, tok, 4 * R), f32),
+            pltpu.SemaphoreType.DMA((tp,)),
+            pltpu.SemaphoreType.DMA((tp,)),
+            pltpu.SemaphoreType.DMA((tp,)),
+            pltpu.SemaphoreType.DMA((tp,)),
+        ],
+        compiler_params=pltpu.CompilerParams(
+            vmem_limit_bytes=48 * 1024 * 1024, collective_id=0, has_side_effects=True
+        ),
     )(got, out_grads, live, match, pick)
-    swapped = lax.all_to_all(parts.reshape(tp, tok, 4 * R), "tp", split_axis=0, concat_axis=0, tiled=True)
-    own_rank = jnp.sum(swapped, axis=0).astype(bf16)
-    rank_values = lax.all_gather(own_rank, "tp", axis=0, tiled=True)
-
-    outgoing = pl.pallas_call(
-        functools.partial(gradient_kernel, *sizes, piece, tok),
-        out_shape=jax.ShapeDtypeStruct((tp, 2 * piece, wide), bf16),
-        scratch_shapes=[pltpu.VMEM((tokens, width), f32)],
-        compiler_params=PARAMS,
-    )(got, out_grads, live, match, pick, columns, rank_values)
     returned = lax.all_to_all(outgoing, "tp", split_axis=0, concat_axis=0, tiled=True)
     return pl.pallas_call(
         functools.partial(unpack_kernel, *sizes),

time: 187 us -> 180 us (0.963)
  blocking collectives: 36.2 us -> 0 us
  Pallas kernels: 7.82 us -> 35.6 us
  waiting for transfers between devices: 79.9 us -> 90.2 us
  local copies, waits for them, and re-layouts: 13.9 us -> 7.36 us
  starting transfers between devices: 16.8 us -> 13.6 us
    reduce_scatter x1, waiting for transfers between devices: 0.01 us -> 28.6 us  [shards(): lax.psum_scatter(frozen_product, 'tp', scatter_dimension=0, tiled=True)]
    pallas_call x2 -> x1, Pallas kernels: 4.98 us -> 31.4 us  [shards(): pl.pallas_call(functools.partial(middle_kernel, *sizes, piece, tok), out_...]
    all_to_all x1 -> x0, blocking collectives: 20.4 us -> none  [shards(): lax.all_to_all(parts.reshape(tp, tok, 4 * R), 'tp', split_axis=0, concat_...]
    all_to_all x1, waiting for transfers between devices: 50.2 us -> 31.6 us  [shards(): lax.all_to_all(outgoing, 'tp', split_axis=0, concat_axis=0, tiled=True)]
    all_gather x1 -> x0, blocking collectives: 15.8 us -> none  [shards(): rank_values = lax.all_gather(own_rank, 'tp', axis=0, tiled=True)]
    unnamed x27 -> x21, local copies, waits for them, and re-layouts: 13.5 us -> 7.02 us
    all_to_all x1, starting transfers between devices: 10 us -> 6.91 us  [shards(): lax.all_to_all(outgoing, 'tp', split_axis=0, concat_axis=0, tiled=True)]
  transfers between devices with their start and end apart: 3 -> 3, of which waited for: 2 -> 3; matrix products, arithmetic and copies ran while one was open for 12% -> 11% of each run, Pallas kernels for 3% -> 18%
where the time goes in v2:
time: 180 us; the launch traced here: 179 us
  waiting for transfers between devices  90.2 us (50%)
  Pallas kernels  35.6 us (20%)
  matrix products  17.9 us (10%)
  between operations  14.2 us (8%)
  starting transfers between devices  13.6 us (8%)
  local copies, waits for them, and re-layouts  7.36 us (4%)
    all_to_all x1, waiting for transfers between devices, shards(): lax.all_to_all(outgoing, 'tp', split_axis=0, concat_axis=0, tiled=True)  31.6 us
    pallas_call x1, Pallas kernels, shards(): pl.pallas_call(functools.partial(middle_kernel, *sizes, piece, tok), out_...  31.4 us
    all_to_all x1, waiting for transfers between devices, shards(): got = lax.all_to_all(packed, 'tp', split_axis=0, concat_axis=0, tiled=True)  30 us
    reduce_scatter x1, waiting for transfers between devices, shards(): lax.psum_scatter(frozen_product, 'tp', scatter_dimension=0, tiled=True)  28.6 us
    dot_general x1, matrix products, shards(): jnp.einsum('ptf,pfd->td', masked, frozen_weights, preferred_element_type=...  17.9 us
    unnamed x21, local copies, waits for them, and re-layouts  7.02 us
    all_to_all x1, starting transfers between devices, shards(): lax.all_to_all(outgoing, 'tp', split_axis=0, concat_axis=0, tiled=True)  6.91 us
    all_to_all x1, starting transfers between devices, shards(): got = lax.all_to_all(packed, 'tp', split_axis=0, concat_axis=0, tiled=True)  6.69 us
  transfers between devices with their start and end apart: 3, of which 3 were waited for; matrix products, arithmetic and copies ran while one was open for 11% of the time, Pallas kernels for 18%

profile of v2, /device:TPU:11, one launch (start us, length us, event | category | flops | bytes accessed | tf_op | source)
XLA Modules:
  0.0 179.4 jit_solution(9576494455755696183)
XLA Ops:
  7.2 0.0 copy-start.1
  7.2 1.4 copy-done.1
  8.6 0.0 copy-start.2
  8.6 1.0 copy-done.2
  9.6 0.0 copy-start.4
  9.6 0.9 copy-done.4
  10.5 1.8 %shard_map.112 = bf16[16,32,2080]{2,1,0:T(8,128)(2,1)} custom-call(bf16[2,16,25600]{2,1,0:T(8,128)(2,1)S(1)} %copy-done.1, bf16[2,16,5120]{2,1,0:T(8,128)(2,1)S(1)} %copy-done.2, bf16[16,5120]{1,0:T(8,128)(2,1)S(1)} %copy-done.4), custom_call_target="tpu_custom_call" | custom-call | tf_op jit(solution)/shard_map/pallas_call | solution.py:181
  12.3 0.0 copy-start.9
  12.3 0.0 copy-start.8
  12.3 0.0 copy-start.5
  12.3 6.7 %all-to-all-start = ((bf16[16,32,2080]{2,1,0:T(8,128)(2,1)}), bf16[16,32,2080]{2,1,0:T(8,128)(2,1)}, u32[]{:S(2)}, u32[]{:S(2)}) async-start(bf16[16,32,2080]{2,1,0:T(8,128)(2,1)} %shard_map.112), calls=%async_computation | async-start | bytes 4456448 | tf_op jit(solution)/shard_map/all_to_all | solution.py:186
  19.0 0.0 reduce-scatter.2.cloned.1.call-start
  19.0 0.0 copy-done.9
  19.0 0.1 slice.6
  19.1 0.1 convert_reduce_fusion
  19.2 0.0 copy-done.8
  19.2 0.1 select_reduce_fusion.2
  19.3 0.0 copy-done.5
  19.3 17.9 %convolution_bitcast_fusion = f32[256,5120]{1,0:T(8,128)} fusion(bf16[2,1600,5120]{2,1,0:T(8,128)(2,1)} %param.11, bf16[2,256,1600]{1,2,0:T(8,128)(2,1)S(1)} %copy-done.5, bf16[256]{0:T(256)(128)(2,1)S(1)} %compare_convert_fusion.2), kind=kOutput, calls=%fused_computation | convolution fusion | flops 8389427200 | bytes 39649792 | tf_op jit(solution)/shard_map/ptf,pfd->td/dot_general | solution.py:206
  37.2 0.0 reduce-scatter.2.cloned.1.call-update
  37.2 0.0 copy-start.6
  37.2 0.0 copy-start.7
  37.2 1.4 copy.21.grads_ref
  38.6 0.1 copy.19
  38.7 0.1 copy.20
  38.9 0.0 copy-done.6
  38.9 0.1 select_reduce_fusion
  39.0 0.0 copy-done.7
  39.0 0.1 select_reduce_fusion.1
  39.1 0.1 fusion.2.pick_ref
  39.2 0.1 compare_convert_fusion.match_ref
  39.3 30.0 %all-to-all-done.got_ref = bf16[16,32,2080]{2,1,0:T(8,128)(2,1)} async-done(((bf16[16,32,2080]{2,1,0:T(8,128)(2,1)}), bf16[16,32,2080]{2,1,0:T(8,128)(2,1)}, u32[]{:S(2)}, u32[]{:S(2)}) %all-to-all-start) | async-done | bytes 2129952 | tf_op jit(solution)/shard_map/all_to_all | solution.py:186
  69.3 31.4 %shard_map.113 = bf16[16,32,2080]{2,1,0:T(8,128)(2,1)S(1)} custom-call(bf16[16,32,2080]{2,1,0:T(8,128)(2,1)} %all-to-all-done.got_ref, bf16[2,256,1600]{2,1,0:T(8,128)(2,1)S(1)} %copy.21.grads_ref, bf16[256,1]{1,0:T(8,128)(2,1)S(1)} %compare_convert_fusion.1.live_ref, f32[256,256]{1,0:T(8,128)S(1)} %compare_convert_fusion.match_ref, ...), custom_call_target="tpu_custom_call" | custom-call | tf_op jit(solution)/shard_map/pallas_call | solution.py:209
  100.7 0.0 copy-start
  100.7 1.4 copy-done
  102.1 6.9 %all-to-all-start.1 = ((bf16[16,32,2080]{2,1,0:T(8,128)(2,1)}), bf16[16,32,2080]{2,1,0:T(8,128)(2,1)S(1)}, u32[]{:S(2)}, u32[]{:S(2)}) async-start(bf16[16,32,2080]{2,1,0:T(8,128)(2,1)} %copy-done), calls=%async_computation.1 | async-start | bytes 4456448 | tf_op jit(solution)/shard_map/all_to_all | solution.py:227
  109.0 28.6 %reduce-scatter.2.cloned.1.call-done.base_ref = f32[16,5120]{1,0:T(8,128)} async-done(((f32[256,5120]{1,0:T(8,128)}), f32[16,5120]{1,0:T(8,128)}) %reduce-scatter.2.cloned.1.call-update) | async-done | bytes 327696 | tf_op jit(solution)/shard_map/reduce_scatter | solution.py:207
  137.6 31.6 %all-to-all-done.1.got_ref = bf16[16,32,2080]{2,1,0:T(8,128)(2,1)S(1)} async-done(((bf16[16,32,2080]{2,1,0:T(8,128)(2,1)}), bf16[16,32,2080]{2,1,0:T(8,128)(2,1)S(1)}, u32[]{:S(2)}, u32[]{:S(2)}) %all-to-all-start.1) | async-done | bytes 2129952 | tf_op jit(solution)/shard_map/all_to_all | solution.py:227
  169.2 0.0 copy-start.3
  169.2 1.0 copy-done.3
  170.1 2.4 %shard_map.114 = (f32[16,5120]{1,0:T(8,128)}, f32[2,16,5120]{2,1,0:T(8,128)}, f32[2,16,25600]{2,1,0:T(8,128)}) custom-call(bf16[16,32,2080]{2,1,0:T(8,128)(2,1)S(1)} %all-to-all-done.1.got_ref, f32[16,5120]{1,0:T(8,128)S(1)} %copy-done.3), custom_call_target="tpu_custom_call" | custom-call | tf_op jit(solution)/shard_map/pallas_call | solution.py:228
  (5 shorter events, 0.1 us)
Async XLA Ops:
  7.2 1.4 copy-start.1
  8.6 1.0 copy-start.2
  9.6 0.9 copy-start.4
  12.3 6.7 %copy-start.9 = (s32[5]{0:T(128)S(1)}, s32[5]{0:T(128)}, u32[]{:S(2)}) copy-start(s32[5]{0:T(128)} %param.16) | copy-start | bytes 64
  12.3 6.9 %copy-start.8 = (s32[4]{0:T(128)S(1)}, s32[4]{0:T(128)}, u32[]{:S(2)}) copy-start(s32[4]{0:T(128)} %param.17) | copy-start | bytes 52
  12.3 7.0 %copy-start.5 = (bf16[2,256,1600]{1,2,0:T(8,128)(2,1)S(1)}, bf16[2,256,1600]{1,2,0:T(8,128)(2,1)}, u32[]{:S(2)}) copy-start(bf16[2,256,1600]{1,2,0:T(8,128)(2,1)} %param.10) | copy-start | bytes 4915204
  12.3 57.0 %all-to-all-start = ((bf16[16,32,2080]{2,1,0:T(8,128)(2,1)}), bf16[16,32,2080]{2,1,0:T(8,128)(2,1)}, u32[]{:S(2)}, u32[]{:S(2)}) async-start(bf16[16,32,2080]{2,1,0:T(8,128)(2,1)} %shard_map.112), calls=%async_computation | async-start | bytes 4456448 | tf_op jit(solution)/shard_map/all_to_all | solution.py:186
  19.0 118.6 %reduce-scatter.2.cloned.1.call-start = ((), (), s32[]{:S(2)}) async-start(), calls=%async_computation.3 | async-start | bytes 5570560 | tf_op jit(solution)/shard_map/reduce_scatter | solution.py:207
  37.2 1.7 copy-start.6
  37.2 1.8 %copy-start.7 = (s32[4]{0:T(128)S(1)}, s32[4]{0:T(128)}, u32[]{:S(2)}) copy-start(s32[4]{0:T(128)} %param.14) | copy-start | bytes 52
  100.7 1.4 copy-start
  102.1 67.1 %all-to-all-start.1 = ((bf16[16,32,2080]{2,1,0:T(8,128)(2,1)}), bf16[16,32,2080]{2,1,0:T(8,128)(2,1)S(1)}, u32[]{:S(2)}, u32[]{:S(2)}) async-start(bf16[16,32,2080]{2,1,0:T(8,128)(2,1)} %copy-done), calls=%async_computation.1 | async-start | bytes 4456448 | tf_op jit(solution)/shard_map/all_to_all | solution.py:227
  169.2 1.0 copy-start.3
Sparse Core Ops, SparseCore 0:
  37.3 100.2 reduce-scatter.1

commit v3 on v2

--- a/solution.py
+++ b/solution.py
@@ -204,7 +204,16 @@
 
     masked = out_grads * live[None]
     frozen_product = jnp.einsum("ptf,pfd->td", masked, frozen_weights, preferred_element_type=f32)
-    frozen_rows = lax.psum_scatter(frozen_product, "tp", scatter_dimension=0, tiled=True)
+    core = lax.axis_index("tp") % 2
+    split = frozen_product.reshape(tp // 2, 2, tok, model)
+    kept = lax.dynamic_index_in_dim(split, core, 1, keepdims=False)
+    given = lax.dynamic_index_in_dim(split, 1 - core, 1, keepdims=False)
+    swap = [(d, d ^ 1) for d in range(tp)]
+    paired = (kept + lax.ppermute(given, "tp", swap)).reshape(tokens // 2, model)
+    groups = [list(range(c, tp, 2)) for c in range(2)]
+    frozen_rows = lax.psum_scatter(
+        paired, "tp", scatter_dimension=0, axis_index_groups=groups, tiled=True
+    )
 
     outgoing = pl.pallas_call(
         functools.partial(middle_kernel, *sizes, piece, tok),

time: 180 us -> 199 us (1.11)
  waiting for transfers between devices: 90.2 us -> 117 us
  Pallas kernels: 35.6 us -> 23.7 us
  other arithmetic: 0.6 us -> 5.62 us
  matrix products: 17.9 us -> 15.8 us
    all_to_all x1, waiting for transfers between devices: 30 us -> 64.5 us  [shards(): got = lax.all_to_all(packed, 'tp', split_axis=0, concat_axis=0, tiled=True)]
    reduce_scatter x1, waiting for transfers between devices: 28.6 us -> 6.31 us  [shards(): lax.psum_scatter(paired, 'tp', scatter_dimension=0, axis_index_groups=gro...]
    all_to_all x1, waiting for transfers between devices: 31.6 us -> 46.2 us  [shards(): lax.all_to_all(outgoing, 'tp', split_axis=0, concat_axis=0, tiled=True)]
    pallas_call x1, Pallas kernels: 31.4 us -> 19.5 us  [shards(): pl.pallas_call(functools.partial(middle_kernel, *sizes, piece, tok), out_...]
    add x0 -> x1, other arithmetic: none -> 4.36 us  [shards(): kept + lax.ppermute(given, 'tp', swap)]
    dot_general x1, matrix products: 17.9 us -> 15.8 us  [shards(): jnp.einsum('ptf,pfd->td', masked, frozen_weights, preferred_element_type=...]
    unnamed x21 -> x19, local copies, waits for them, and re-layouts: 7.02 us -> 5.93 us
  transfers between devices with their start and end apart: 3 -> 4, of which waited for: 3 -> 3; matrix products, arithmetic and copies ran while one was open for 11% -> 3% of each run, Pallas kernels for 18% -> 11%
where the time goes in v3:
time: 199 us
  waiting for transfers between devices  117 us (59%)
  Pallas kernels  23.7 us (12%)
  matrix products  15.8 us (8%)
  between operations  14.2 us (7%)
  starting transfers between devices  13.6 us (7%)
  local copies, waits for them, and re-layouts  8.61 us (4%)
  other arithmetic  5.62 us (3%)
    all_to_all x1, waiting for transfers between devices, shards(): got = lax.all_to_all(packed, 'tp', split_axis=0, concat_axis=0, tiled=True)  64.5 us
    all_to_all x1, waiting for transfers between devices, shards(): lax.all_to_all(outgoing, 'tp', split_axis=0, concat_axis=0, tiled=True)  46.2 us
    pallas_call x1, Pallas kernels, shards(): pl.pallas_call(functools.partial(middle_kernel, *sizes, piece, tok), out_...  19.5 us
    dot_general x1, matrix products, shards(): jnp.einsum('ptf,pfd->td', masked, frozen_weights, preferred_element_type=...  15.8 us
    all_to_all x1, starting transfers between devices, shards(): lax.all_to_all(outgoing, 'tp', split_axis=0, concat_axis=0, tiled=True)  6.8 us
    reduce_scatter x1, waiting for transfers between devices, shards(): lax.psum_scatter(paired, 'tp', scatter_dimension=0, axis_index_groups=gro...  6.31 us
    all_to_all x1, starting transfers between devices, shards(): got = lax.all_to_all(packed, 'tp', split_axis=0, concat_axis=0, tiled=True)  6.13 us
    unnamed x19, local copies, waits for them, and re-layouts  5.93 us
  transfers between devices with their start and end apart: 4, of which 3 were waited for; matrix products, arithmetic and copies ran while one was open for 3% of the time, Pallas kernels for 11%

profile of v3, /device:TPU:11, one launch (start us, length us, event | category | flops | bytes accessed | tf_op | source)
XLA Modules:
  0.0 198.6 jit_solution(4044967412408272171)
XLA Ops:
  7.2 0.7 slice.6
  7.9 0.1 convert_reduce_fusion
  8.0 0.8 select_reduce_fusion.2
  8.8 15.8 %fusion = f32[256,5120,1]{1,0,2:T(8,128)S(1)} fusion(bf16[2,1600,5120]{2,1,0:T(8,128)(2,1)} %param.11, bf16[2,256,1600]{1,2,0:T(8,128)(2,1)} %param.10, bf16[256]{0:T(256)(128)(2,1)S(1)} %compare_convert_fusion.2), kind=kOutput, calls=%fused_computation.2 | convolution fusion | flops 8389427200 | bytes 39649792 | tf_op jit(solution)/shard_map/ptf,pfd->td/dot_general | solution.py:206
  24.6 0.0 copy-start.5
  24.6 0.0 copy-start.1
  24.6 0.0 copy-start.2
  24.6 0.0 copy-start.4
  24.6 1.7 dynamic-slice_bitcast_fusion
  26.3 1.6 copy-done.5
  27.9 0.7 collective-permute-start
  28.5 0.0 copy-done.1
  28.5 0.0 copy-done.2
  28.6 0.0 copy-done.4
  28.6 1.8 shard_map.112
  30.3 0.0 copy-start.6
  30.3 6.1 %all-to-all-start = ((bf16[16,32,2080]{2,1,0:T(8,128)(2,1)}), bf16[16,32,2080]{2,1,0:T(8,128)(2,1)}, u32[]{:S(2)}, u32[]{:S(2)}) async-start(bf16[16,32,2080]{2,1,0:T(8,128)(2,1)} %shard_map.112), calls=%async_computation | async-start | bytes 4456448 | tf_op jit(solution)/shard_map/all_to_all | solution.py:186
  36.5 0.0 reduce-scatter.2.cloned.1.call-start
  36.5 0.0 copy-done.6
  36.5 1.4 copy.21.grads_ref
  37.9 0.1 copy.19
  38.0 0.1 copy.20
  38.2 0.0 collective-permute-done
  38.2 4.4 %bitcast_add_fusion = f32[8,16,5120]{2,1,0:T(8,128)} fusion(f32[8,16,5120]{2,1,0:T(8,128)} %collective-permute-done, f32[8,2,16,5120]{3,2,1,0:T(8,128)} %bitcast.13, s32[]{:T(128)S(6)} %select_n.71), kind=kLoop, calls=%fused_computation | loop fusion | flops 655360 | bytes 7864324 | tf_op jit(solution)/shard_map/add | solution.py:212
  42.6 0.0 copy-start.7
  42.6 0.0 copy-start.8
  42.6 0.0 reduce-scatter.2.cloned.1.call-update
  42.6 0.6 copy-done.7
  43.2 0.1 select_reduce_fusion
  43.3 0.0 copy-done.8
  43.3 0.1 select_reduce_fusion.1
  43.4 0.1 fusion.3.pick_ref
  43.5 0.1 compare_convert_fusion.match_ref
  43.7 64.5 %all-to-all-done.got_ref = bf16[16,32,2080]{2,1,0:T(8,128)(2,1)} async-done(((bf16[16,32,2080]{2,1,0:T(8,128)(2,1)}), bf16[16,32,2080]{2,1,0:T(8,128)(2,1)}, u32[]{:S(2)}, u32[]{:S(2)}) %all-to-all-start) | async-done | bytes 2129952 | tf_op jit(solution)/shard_map/all_to_all | solution.py:186
  108.2 19.5 %shard_map.113 = bf16[16,32,2080]{2,1,0:T(8,128)(2,1)S(1)} custom-call(bf16[16,32,2080]{2,1,0:T(8,128)(2,1)} %all-to-all-done.got_ref, bf16[2,256,1600]{2,1,0:T(8,128)(2,1)S(1)} %copy.21.grads_ref, bf16[256,1]{1,0:T(8,128)(2,1)S(1)} %compare_convert_fusion.1.live_ref, f32[256,256]{1,0:T(8,128)S(1)} %compare_convert_fusion.match_ref, ...), custom_call_target="tpu_custom_call" | custom-call | tf_op jit(solution)/shard_map/pallas_call | solution.py:218
  127.7 0.0 copy-start
  127.7 1.4 copy-done
  129.1 6.8 %all-to-all-start.1 = ((bf16[16,32,2080]{2,1,0:T(8,128)(2,1)}), bf16[16,32,2080]{2,1,0:T(8,128)(2,1)S(1)}, u32[]{:S(2)}, u32[]{:S(2)}) async-start(bf16[16,32,2080]{2,1,0:T(8,128)(2,1)} %copy-done), calls=%async_computation.1 | async-start | bytes 4456448 | tf_op jit(solution)/shard_map/all_to_all | solution.py:236
  135.9 6.3 %reduce-scatter.2.cloned.1.call-done.base_ref = f32[16,5120]{1,0:T(8,128)} async-done(((f32[128,5120]{1,0:T(8,128)}), f32[16,5120]{1,0:T(8,128)}) %reduce-scatter.2.cloned.1.call-update) | async-done | bytes 327696 | tf_op jit(solution)/shard_map/reduce_scatter | solution.py:214
  142.2 46.2 %all-to-all-done.1.got_ref = bf16[16,32,2080]{2,1,0:T(8,128)(2,1)S(1)} async-done(((bf16[16,32,2080]{2,1,0:T(8,128)(2,1)}), bf16[16,32,2080]{2,1,0:T(8,128)(2,1)S(1)}, u32[]{:S(2)}, u32[]{:S(2)}) %all-to-all-start.1) | async-done | bytes 2129952 | tf_op jit(solution)/shard_map/all_to_all | solution.py:236
  188.4 0.0 copy-start.3
  188.4 1.0 copy-done.3
  189.4 2.4 %shard_map.114 = (f32[16,5120]{1,0:T(8,128)}, f32[2,16,5120]{2,1,0:T(8,128)}, f32[2,16,25600]{2,1,0:T(8,128)}) custom-call(bf16[16,32,2080]{2,1,0:T(8,128)(2,1)S(1)} %all-to-all-done.1.got_ref, f32[16,5120]{1,0:T(8,128)S(1)} %copy-done.3), custom_call_target="tpu_custom_call" | custom-call | tf_op jit(solution)/shard_map/pallas_call | solution.py:237
  (5 shorter events, 0.1 us)
Async XLA Ops:
  24.6 3.3 %copy-start.5 = (f32[256,5120,1]{1,0,2:T(8,128)}, f32[256,5120,1]{1,0,2:T(8,128)S(1)}, u32[]{:S(2)}) copy-start(f32[256,5120,1]{1,0,2:T(8,128)S(1)} %fusion) | copy-start | bytes 15728644
  24.6 4.0 %copy-start.1 = (bf16[2,16,25600]{2,1,0:T(8,128)(2,1)S(1)}, bf16[2,16,25600]{2,1,0:T(8,128)(2,1)}, u32[]{:S(2)}) copy-start(bf16[2,16,25600]{2,1,0:T(8,128)(2,1)} %second_ref.1) | copy-start | bytes 4915204
  24.6 4.0 %copy-start.2 = (bf16[2,16,5120]{2,1,0:T(8,128)(2,1)S(1)}, bf16[2,16,5120]{2,1,0:T(8,128)(2,1)}, u32[]{:S(2)}) copy-start(bf16[2,16,5120]{2,1,0:T(8,128)(2,1)} %first_ref.1) | copy-start | bytes 983044
  24.6 4.0 %copy-start.4 = (bf16[16,5120]{1,0:T(8,128)(2,1)S(1)}, bf16[16,5120]{1,0:T(8,128)(2,1)}, u32[]{:S(2)}) copy-start(bf16[16,5120]{1,0:T(8,128)(2,1)} %inputs_ref.1) | copy-start | bytes 491524
  27.9 10.3 %collective-permute-start = (f32[8,16,5120]{2,1,0:T(8,128)}, f32[8,16,5120]{2,1,0:T(8,128)}, u32[]{:S(2)}, u32[]{:S(2)}) collective-permute-start(f32[8,16,5120]{2,1,0:T(8,128)} %dynamic-slice_bitcast_fusion), channel_id=1, source_target_pairs={{0,1},{1,0},{2,3},{3,2},{4,5},{5,4},{6,7},{7,6},{8,9},{9,8},{10,11... | collective-permute-start | bytes 7864328 | tf_op jit(solution)/shard_map/ppermute | solution.py:212
  30.3 6.2 %copy-start.6 = (bf16[2,256,1600]{1,2,0:T(8,128)(2,1)S(1)}, bf16[2,256,1600]{1,2,0:T(8,128)(2,1)}, u32[]{:S(2)}) copy-start(bf16[2,256,1600]{1,2,0:T(8,128)(2,1)} %param.10) | copy-start | bytes 4915204
  30.3 77.8 %all-to-all-start = ((bf16[16,32,2080]{2,1,0:T(8,128)(2,1)}), bf16[16,32,2080]{2,1,0:T(8,128)(2,1)}, u32[]{:S(2)}, u32[]{:S(2)}) async-start(bf16[16,32,2080]{2,1,0:T(8,128)(2,1)} %shard_map.112), calls=%async_computation | async-start | bytes 4456448 | tf_op jit(solution)/shard_map/all_to_all | solution.py:186
  36.5 105.7 %reduce-scatter.2.cloned.1.call-start = ((), (), s32[]{:S(2)}) async-start(), calls=%async_computation.3 | async-start | bytes 2949120 | tf_op jit(solution)/shard_map/reduce_scatter | solution.py:214
  42.6 0.7 copy-start.7
  42.6 0.8 copy-start.8
  127.7 1.4 copy-start
  129.1 59.3 %all-to-all-start.1 = ((bf16[16,32,2080]{2,1,0:T(8,128)(2,1)}), bf16[16,32,2080]{2,1,0:T(8,128)(2,1)S(1)}, u32[]{:S(2)}, u32[]{:S(2)}) async-start(bf16[16,32,2080]{2,1,0:T(8,128)(2,1)} %copy-done), calls=%async_computation.1 | async-start | bytes 4456448 | tf_op jit(solution)/shard_map/all_to_all | solution.py:236
  188.4 1.0 copy-start.3
Sparse Core Ops, SparseCore 0:
  42.7 99.4 reduce-scatter.1
